TPU v7x, 128 devices: a whole 4x4x4 slice. The times are simulated.
128 devices in a mesh: dp: 4 (over z), ctx: 4 (over y), tensor: 8 (over x, core).
Axes of the slice: x: 4, y: 4, z: 4, core: 2. Of those that a mesh axis runs over, the one named last changes fastest.
Arguments:
- query_rows: bfloat16 [4, 512, 4096], P('dp', 'ctx', 'tensor'), may hold values from -200 to 200
- key_rows: bfloat16 [4, 512, 256], P('dp', 'ctx'), may hold values from -6 to 6
- value_rows: bfloat16 [4, 512, 256], P('dp', 'ctx'), may hold values from -6 to 6
- residual: bfloat16 [4, 512, 4096], P('dp', ('ctx', 'tensor')), may hold values from -6 to 6
- out_proj: bfloat16 [4096, 4096], P('tensor'), may hold values from -0.09375 to 0.09375
- post_gain: bfloat16 [4096], replicated, may hold values from 0.099609375 to 1.8984375
- router: bfloat16 [4096, 64], replicated, may hold values from -10 to 10
- routes: int32 [4, 512, 8], P('dp', ('ctx', 'tensor')), may hold values from 0 to 63, all different within a row; in each aligned block of 16 rows (0 to 15, 16 to 31, ..., all dimensions but the last counted through in order) at most 4 rows name the same one
- w_gate: bfloat16 [64, 4096, 1536], P(('ctx', 'tensor'), None, 'dp'), may hold values from -0.09375 to 0.09375
- w_up: bfloat16 [64, 4096, 1536], P(('ctx', 'tensor'), None, 'dp'), may hold values from -0.09375 to 0.09375
- w_down: bfloat16 [64, 1536, 4096], P(('ctx', 'tensor'), 'dp'), may hold values from -80 to 80
Outputs:
- layer_out: bfloat16 [4, 512, 4096], P('dp', ('ctx', 'tensor'))
Inputs may be any that keep to these rules, and one draw needn't show every extreme that they name: `routes`: the 8 experts of a token differ. Among the 16 tokens of one device (aligned blocks of the token rows), no expert is named by more than 4 of them, a bound that some block reaches.
All inputs are finite; a program needn't handle non-finite values.
Results may differ from a plain program's by a relative error of at most 0.014.
Values may be sent and summed in bfloat16 or wider, within the bound.
A program may use at most 128 MiB of HBM per device.

v0:
```python
import functools

import jax
import jax.numpy as jnp
import numpy as np
from jax import lax
from jax.experimental import pallas as pl
from jax.experimental.pallas import tpu as pltpu
from jax.sharding import PartitionSpec as P

MESH = pl.DeviceIdType.MESH
F32 = jnp.float32
BF16 = jnp.bfloat16

D = 4096
HEAD = 128
HEADS = 4
SEQ = 512
LOCAL = 128
TOK = 16
EXPERTS = 64
FF = 384
CAP = 4
GATES = 128
WIDE = D + GATES
W = WIDE // 3
GROUP = 256
SLOTS = TOK * CAP

ORDER = (("x", "y", "z"), ("y", "z", "x"), ("z", "x", "y"))
PARTS = range(3)
AG_ROUNDS = ((0, 512), (512, 512), (1024, 384))
RS_ROUNDS = ((0, 384), (384, 512), (896, 512))
VMEM = 63 * 2**20


def rope_tables():
    half = HEAD // 2
    places = np.arange(SEQ).astype(np.float32)
    freqs = np.power(
        np.float32(1000000.0), -(np.arange(half).astype(np.float32) * np.float32(2.0) / np.float32(HEAD))
    ).astype(np.float32)
    angles = (places[:, None] * freqs[None, :]).astype(np.float32)
    cosine, sine = np.cos(angles), np.sin(angles)
    return (
        np.concatenate([cosine, cosine], axis=1).astype(np.float32),
        np.concatenate([-sine, sine], axis=1).astype(np.float32),
    )


def place():
    t = lax.axis_index("tensor")
    return {"x": t // 2, "y": lax.axis_index("ctx"), "z": lax.axis_index("dp")}, t % 2


def device(me, k, axis, step):
    value = (me[axis] + step) % 4
    if axis == "x":
        return {"tensor": value * 2 + k}
    return {"ctx" if axis == "y" else "dp": value}


def sibling(me, k):
    return {"tensor": me["x"] * 2 + 1 - k}


def greet(me, k, axes):
    barrier = pltpu.get_barrier_semaphore()
    for axis in axes:
        for step in (1, 2, 3):
            pl.semaphore_signal(
                barrier, inc=1, device_id=device(me, k, axis, step), device_id_type=MESH
            )
    pl.semaphore_signal(barrier, inc=1, device_id=sibling(me, k), device_id_type=MESH)
    pl.semaphore_wait(barrier, 3 * len(axes) + 1)


def send(src, dst, to, send_sem, recv_sem):
    pltpu.make_async_remote_copy(
        src_ref=src,
        dst_ref=dst,
        send_sem=send_sem,
        recv_sem=recv_sem,
        device_id=to,
        device_id_type=MESH,
    ).start()


def wait(ref, sem):
    pltpu.make_async_copy(ref, ref, sem).wait()


def turn(values, cosine, sine):
    values = values.astype(F32)
    return (values * cosine + pltpu.roll(values, HEAD // 2, 1) * sine).astype(BF16)


def front_kernel(
    query_ref, key_ref, value_ref, residual_ref, proj_hbm, gain_ref, router_ref, routes_ref,
    cos_ref, sin_ref, rows_ref, mixed_ref,
    proj, kv, qrot, krot, partial, far, from_sibling, from_ring,
    proj_sem, kv_send, kv_recv, sib_send, sib_recv, ring_send, ring_recv,
):
    me, k = place()
    t = lax.axis_index("tensor")
    y = me["y"]
    load = pltpu.make_async_copy(proj_hbm, proj, proj_sem)
    load.start()
    head = pl.multiple_of((t // 4) * HEAD, HEAD)
    kv[y, 0] = key_ref[0, :, pl.ds(head, HEAD)]
    kv[y, 1] = value_ref[0, :, pl.ds(head, HEAD)]
    greet(me, k, "xy")
    for step in (1, 2, 3):
        send(kv.at[y], kv.at[y], device(me, k, "y", step), kv_send, kv_recv)
    own = pl.ds(pl.multiple_of(y * LOCAL, LOCAL), LOCAL)
    cosine, sine = cos_ref[own, :], sin_ref[own, :]
    for h in range(HEADS):
        qrot[pl.ds(h * LOCAL, LOCAL), :] = turn(query_ref[0, :, h * HEAD : (h + 1) * HEAD], cosine, sine)
    wait(kv.at[pl.ds(0, 3)], kv_recv)
    for c in range(4):
        span = pl.ds(c * LOCAL, LOCAL)
        krot[span, :] = turn(kv[c, 0], cos_ref[span, :], sin_ref[span, :])
    values = kv[:, 1].reshape(SEQ, HEAD)
    place_q = y * LOCAL + lax.broadcasted_iota(jnp.int32, (LOCAL, SEQ), 0)
    causal = place_q >= lax.broadcasted_iota(jnp.int32, (LOCAL, SEQ), 1)
    attended = []
    for h in range(HEADS):
        score = lax.dot_general(
            qrot[pl.ds(h * LOCAL, LOCAL), :], krot[...], (((1,), (1,)), ((), ())),
            preferred_element_type=F32,
        ) / jnp.sqrt(F32(HEAD))
        score = jnp.where(causal, score, F32(-1e30))
        peak = jnp.max(score, axis=-1, keepdims=True)
        expon = jnp.where(causal, jnp.exp(score - peak), F32(0.0))
        total = jnp.sum(expon, axis=-1, keepdims=True)
        summed = jnp.dot(expon.astype(BF16), values, preferred_element_type=F32)
        attended.append((summed / total).astype(BF16))
    attended = jnp.concatenate(attended, axis=1)
    load.wait()
    for c in range(8):
        cols = slice(c * 512, (c + 1) * 512)
        out = jnp.dot(attended, proj[:, cols], preferred_element_type=F32)
        partial[:, :, :, cols] = out.reshape(4, 2, TOK, 512)
        far[:, :, cols] = partial[:, 1 - k, :, cols].astype(BF16)
    to = sibling(me, k)
    send(far, from_sibling, to, sib_send, sib_recv)
    wait(far, sib_send)
    wait(from_sibling, sib_recv)
    for step in (2, 1, 3):
        v = (me["x"] + step) % 4
        far[v] = (partial[v, k] + from_sibling[v].astype(F32)).astype(BF16)
        send(far.at[v], from_ring.at[step - 1], device(me, k, "x", step), ring_send, ring_recv)
    own_sum = partial[me["x"], k] + from_sibling[me["x"]].astype(F32)
    wait(from_ring, ring_recv)
    projected = own_sum + from_ring[0].astype(F32) + from_ring[1].astype(F32) + from_ring[2].astype(F32)
    mixed = (residual_ref[0].astype(F32) + projected).astype(BF16)
    mixed_ref[...] = mixed
    wide = mixed.astype(F32)
    scale = lax.rsqrt(jnp.mean(wide * wide, axis=-1, keepdims=True) + 1e-06)
    normed = (wide * scale * gain_ref[...].astype(F32)).astype(BF16)
    rows_ref[:, GATES:] = normed
    logits = jnp.dot(normed, router_ref[...], preferred_element_type=F32)
    lane = lax.broadcasted_iota(jnp.int32, (TOK, EXPERTS), 1)
    routes = routes_ref[0]
    chosen = routes[:, 0:1] == lane
    for j in range(1, 8):
        chosen = jnp.logical_or(chosen, routes[:, j : j + 1] == lane)
    peak = jnp.max(jnp.where(chosen, logits, F32(-3e38)), axis=-1, keepdims=True)
    expon = jnp.where(chosen, jnp.exp(logits - peak), F32(0.0))
    gates = expon / jnp.sum(expon, axis=-1, keepdims=True)
    high = gates.astype(BF16).astype(F32)
    rows_ref[:, :GATES] = jnp.concatenate([high, gates - high], axis=1).astype(BF16)
    wait(kv.at[pl.ds(0, 3)], kv_send)
    wait(from_ring, ring_send)


def front(query_rows, key_rows, value_rows, residual, out_proj, post_gain, router, routes):
    cosine, sine = rope_tables()
    vmem = pl.BlockSpec(memory_space=pltpu.VMEM)
    dma = pltpu.SemaphoreType.DMA
    return pl.pallas_call(
        front_kernel,
        out_shape=(
            jax.ShapeDtypeStruct((TOK, WIDE), BF16),
            jax.ShapeDtypeStruct((TOK, D), BF16),
        ),
        in_specs=[vmem] * 4 + [pl.BlockSpec(memory_space=pl.ANY)] + [vmem] * 5,
        out_specs=(vmem, vmem),
        scratch_shapes=[
            pltpu.VMEM((HEADS * HEAD, D), BF16),
            pltpu.VMEM((4, 2, LOCAL, HEAD), BF16),
            pltpu.VMEM((HEADS * LOCAL, HEAD), BF16),
            pltpu.VMEM((SEQ, HEAD), BF16),
            pltpu.VMEM((4, 2, TOK, D), F32),
            pltpu.VMEM((4, TOK, D), BF16),
            pltpu.VMEM((4, TOK, D), BF16),
            pltpu.VMEM((3, TOK, D), BF16),
            dma, dma, dma, dma, dma, dma, dma,
        ],
        compiler_params=pltpu.CompilerParams(
            collective_id=0, has_side_effects=True, vmem_limit_bytes=48 * 2**20
        ),
    )(
        query_rows, key_rows, value_rows, residual, out_proj, post_gain.reshape(1, D), router, routes,
        jnp.asarray(cosine), jnp.asarray(sine),
    )


def expert_kernel(
    rows_ref, mixed_ref, gate_hbm, up_hbm, down_hbm, out_ref,
    x0, x1, x2, rd0, rd1, rd2, rf0, rf1, rf2, rr0, rr1, rr2, rb0, rb1, rb2, ra0, ra1, ra2,
    wgu, wd, packed, acc, hidden, pick, unpick, row_gate,
    w_sem, p1s, p1r, p2s, p2r, p3s, p3r, ds, dr,
    qds, qdr, qfs, qfr, q3s, q3r, q2s, q2r, q1s, q1r,
):
    xs, rd, rf, rr = (x0, x1, x2), (rd0, rd1, rd2), (rf0, rf1, rf2), (rr0, rr1, rr2)
    rb, ra = (rb0, rb1, rb2), (ra0, ra1, ra2)
    me, k = place()
    twin = sibling(me, k)

    loads = []
    for e in range(2):
        loads.append(pltpu.make_async_copy(gate_hbm.at[e], wgu.at[e, :, pl.ds(0, FF)], w_sem.at[e]))
        loads.append(pltpu.make_async_copy(up_hbm.at[e], wgu.at[e, :, pl.ds(FF, FF)], w_sem.at[2 + e]))
    loads.append(pltpu.make_async_copy(down_hbm, wd, w_sem.at[4]))
    for load in loads:
        load.start()
    for p in PARTS:
        xs[p][k, me["z"], me["y"], me["x"]] = rows_ref[:, p * W : (p + 1) * W]
    greet(me, k, "xyz")

    def at(ref, lead, cols, fix):
        index = [fix.get(axis, slice(None)) for axis in "zyx"]
        return ref.at[(*lead, *index, slice(None), pl.ds(*cols))]


    def p1_start(p):
        a = ORDER[p][0]
        block = at(xs[p], (k,), (0, W), me)
        for step in (2, 1, 3):
            send(block, block, device(me, k, a, step), p1s.at[p], p1r.at[p])

    def p1_wait(p):
        wait(xs[p].at[0, 0, 0, pl.ds(0, 3)], p1r.at[p])

    def p2_start(p, r):
        a, b, c = ORDER[p]
        unit = at(xs[p], (k,), AG_ROUNDS[r], {b: me[b], c: me[c]})
        for step in (2, 1, 3):
            send(unit, unit, device(me, k, b, step), p2s.at[p, r], p2r.at[p, r])

    def p2_bytes(p, r):
        return xs[p].at[0, 0, pl.ds(0, 3), :, :, pl.ds(*AG_ROUNDS[r])]

    def p3_unit(p, r, step, half=None):
        a, b, c = ORDER[p]
        fix = {c: (me[c] + step) % 4}
        if half is not None:
            fix[b] = pl.ds(2 * half, 2)
        return at(xs[p], (k,), AG_ROUNDS[r], fix)

    def p3_send(p, r, step, half, way):
        unit = p3_unit(p, r, step, half)
        recv = p3r.at[p, r, 2] if half is not None else p3r.at[p, r, 0 if way == 1 else 1]
        send(unit, unit, device(me, k, ORDER[p][2], way), p3s.at[p, r], recv)

    def twin_send(p, r, step):
        unit = p3_unit(p, r, step)
        send(unit, unit, twin, ds.at[p, r], dr.at[p, r])

    def p3_start(r):
        for p in PARTS:
            wait(p2_bytes(p, r), p2r.at[p, r])
            p3_send(p, r, 0, None, 1)
            p3_send(p, r, 0, None, -1)

    def p3_forward(r):
        for p in PARTS:
            wait(p3_unit(p, r, -1), p3r.at[p, r, 0])
            p3_send(p, r, -1, 0, 1)
            wait(p3_unit(p, r, 1), p3r.at[p, r, 1])
            p3_send(p, r, 1, 1, -1)
        for p in PARTS:
            for step in (0, -1, 1):
                twin_send(p, r, step)

    def p3_finish(r):
        for p in PARTS:
            wait(p3_unit(p, r, 2), p3r.at[p, r, 2])
            twin_send(p, r, 2)

    def twin_wait(r):
        for p in PARTS:
            wait(xs[p].at[1 - k, :, :, :, :, pl.ds(*AG_ROUNDS[r])], dr.at[p, r])


    def selections():
        first = 2 * (me["y"] * 8 + lax.axis_index("tensor"))
        rows = lax.broadcasted_iota(jnp.int32, (8, GATES), 0)
        lanes = lax.broadcasted_iota(jnp.int32, (8, GATES), 1)
        mine = jnp.logical_and(lanes % EXPERTS == first + rows, rows < 2).astype(F32).astype(BF16)
        s = lax.broadcasted_iota(jnp.int32, (GROUP, GROUP), 0)
        u = lax.broadcasted_iota(jnp.int32, (GROUP, GROUP), 1)
        earlier = jnp.logical_and(s // TOK == u // TOK, s < u).astype(F32).astype(BF16)
        base = (lax.broadcasted_iota(jnp.int32, (1, GROUP), 1) // TOK * CAP).astype(F32)
        slots = lax.broadcasted_iota(jnp.int32, (SLOTS, GROUP), 0).astype(F32)

        def one(g, carry):
            tile = x0[g // 4, g % 4, :, :, :, :GATES].reshape(GROUP, GATES)
            gate = lax.dot_general(mine, tile, (((1,), (1,)), ((), ())), preferred_element_type=F32)
            named = (gate > 0).astype(F32)
            rank = jnp.dot(named.astype(BF16), earlier, preferred_element_type=F32)
            both = []
            for e in range(2):
                hit = jnp.logical_and(slots == rank[e : e + 1] + base, gate[e : e + 1] > 0).astype(F32)
                worth = jnp.sum(hit * gate[e : e + 1], axis=1, keepdims=True)
                row_gate[e, pl.ds(g * SLOTS, SLOTS), :] = jnp.broadcast_to(worth, (SLOTS, 128))
                both.append(hit)
            both = jnp.concatenate(both, axis=0)
            pick[g] = both.astype(BF16)
            unpick[g] = both.T.astype(BF16)
            return carry

        lax.fori_loop(0, 8, one, 0)

    def spans(r):
        found, at_col = [], 0
        for p in PARTS:
            lo, size = AG_ROUNDS[r]
            if p == 0 and lo == 0:
                lo, size = GATES, size - GATES
            found.append((p, lo, size, at_col))
            at_col += size
        return found

    def compact(r):
        for p, lo, size, col in spans(r):
            def one(g, carry, p=p, lo=lo, size=size, col=col):
                tokens = xs[p][g // 4, g % 4, :, :, :, lo : lo + size].reshape(GROUP, size)
                rows = jnp.dot(pick[g], tokens, preferred_element_type=F32).astype(BF16)
                for e in range(2):
                    packed[e, pl.ds(g * SLOTS, SLOTS), col : col + size] = rows[e * SLOTS : (e + 1) * SLOTS]
                return carry

            lax.fori_loop(0, 8, one, 0)

    def gate_up(r):
        def one(e, carry):
            total = None
            for p, lo, size, col in spans(r):
                from_row = p * W + lo - GATES
                term = jnp.dot(
                    packed[e, :, col : col + size], wgu[e, from_row : from_row + size, :],
                    preferred_element_type=F32,
                )
                total = term if total is None else total + term
            if r > 0:
                total = total + acc[e]
            if r < len(AG_ROUNDS) - 1:
                acc[e] = total
            else:
                gate, up = total[:, :FF], total[:, FF:]
                hidden[e] = (gate / (1.0 + jnp.exp(-gate)) * up).astype(BF16)
            return carry

        lax.fori_loop(0, 2, one, 0)


    def out_cols(p, r):
        lo, size = RS_ROUNDS[r]
        if p == 0 and lo == 0:
            lo, size = GATES, size - GATES
        return lo, size

    def down(r):
        for p in PARTS:
            lo, size = out_cols(p, r)
            col = p * W + lo - GATES

            def product(e, carry, lo=lo, size=size, col=col):
                part = jnp.dot(hidden[e], wd[e, :, col : col + size], preferred_element_type=F32)
                packed[e, :, :size] = (part * row_gate[e, :, 0:1]).astype(BF16)
                return carry

            lax.fori_loop(0, 2, product, 0)

            def one(i, carry, p=p, lo=lo, size=size):
                g = (i + 4 * (1 - k)) % 8
                rows = jnp.concatenate(
                    [packed[e, pl.ds(g * SLOTS, SLOTS), :size] for e in range(2)], axis=0
                )
                tokens = jnp.dot(unpick[g], rows, preferred_element_type=F32).astype(BF16)
                xs[p][g // 4, g % 4, :, :, :, lo : lo + size] = tokens.reshape(4, 4, TOK, size)
                return carry

            lax.fori_loop(0, 4, one, 0)
            cols = (lo, size)
            send(at(xs[p], (1 - k,), cols, {}), at(rd[p], (), cols, {}), twin, qds.at[p, r], qdr.at[p, r])
            lax.fori_loop(4, 8, one, 0)

    def total_into(dst, refs):
        total = refs[0][...].astype(F32)
        for ref in refs[1:]:
            total = total + ref[...].astype(F32)
        dst[...] = total.astype(BF16)

    def unit_of(ref, lead, p, r, step, pieces=1, piece=0):
        a, b, c = ORDER[p]
        fix = {c: (me[c] + step) % 4}
        if pieces == 2:
            fix[b] = pl.ds(2 * piece, 2)
        elif pieces == 4:
            fix[b] = piece
        return at(ref, lead, out_cols(p, r), fix)

    def add_unit(p, r, step):
        def one(i, carry):
            mine = unit_of(xs[p], (k,), p, r, step, 4, i)
            total_into(mine, [mine, unit_of(rd[p], (), p, r, step, 4, i)])
            return carry

        lax.fori_loop(0, 4, one, 0)

    def piece_of(ref, lead, p, r, fix):
        a, b, c = ORDER[p]
        index = [fix.get(axis, slice(None)) for axis in "zyx" if axis != c]
        return ref.at[(*lead, *index, slice(None), pl.ds(*out_cols(p, r)))]

    def halves(p, half):
        return 2 * half

    def s1(r):
        for p in PARTS:
            cols = out_cols(p, r)
            wait(at(rd[p], (), cols, {}), qdr.at[p, r])
            add_unit(p, r, 2)
            c = ORDER[p][2]
            for half, way in ((0, 1), (1, -1)):
                src = unit_of(xs[p], (k,), p, r, 2, 2, half)
                send(src, half_slot(p, r, half), device(me, k, c, way), qfs.at[p, r], qfr.at[p, r, half])
            add_unit(p, r, 1)
            add_unit(p, r, -1)

    def half_slot(p, r, half, i=None):
        b = ORDER[p][1]
        fix = {} if i is None else {b: i}
        a, b, c = ORDER[p]
        index = [fix.get(axis, slice(None)) for axis in "zyx" if axis != c]
        return rf[p].at[(half, *index, slice(None), pl.ds(*out_cols(p, r)))]

    def s2(r):
        for p in PARTS:
            c = ORDER[p][2]
            for half, way in ((0, 1), (1, -1)):
                wait(half_slot(p, r, half), qfr.at[p, r, half])

                def one(i, carry, half=half, way=way):
                    mine = unit_of(xs[p], (k,), p, r, way, 4, 2 * half + i)
                    total_into(mine, [mine, half_slot(p, r, half, i)])
                    return carry

                lax.fori_loop(0, 2, one, 0)
                src = unit_of(xs[p], (k,), p, r, way)
                slot = piece_of(rr[p], (half,), p, r, {})
                send(src, slot, device(me, k, c, way), q3s.at[p, r], q3r.at[p, r])
            add_unit(p, r, 0)

    def s3(r):
        for p in PARTS:
            a, b, c = ORDER[p]
            wait(piece_of(rr[p], (slice(None),), p, r, {}), q3r.at[p, r])

            def one(i, carry, b=b):
                mine = unit_of(xs[p], (k,), p, r, 0, 4, i)
                total_into(mine, [mine] + [piece_of(rr[p], (h,), p, r, {b: i}) for h in range(2)])
                return carry

            lax.fori_loop(0, 4, one, 0)
            for step in (2, 1, 3):
                src = unit_of(xs[p], (k,), p, r, 0, 4, (me[b] + step) % 4)
                slot = rb[p].at[step - 1, :, :, pl.ds(*out_cols(p, r))]
                send(src, slot, device(me, k, b, step), q2s.at[p, r], q2r.at[p, r])

    def s4(r):
        for p in PARTS:
            a, b, c = ORDER[p]
            cols = pl.ds(*out_cols(p, r))
            wait(rb[p].at[:, :, :, cols], q2r.at[p, r])
            mine = unit_of(xs[p], (k,), p, r, 0, 4, me[b])
            total_into(mine, [mine] + [rb[p].at[j, :, :, cols] for j in range(3)])
            for step in (2, 1, 3):
                src = at(xs[p], (k,), out_cols(p, r), {**me, a: (me[a] + step) % 4})
                send(src, ra[p].at[step - 1, :, cols], device(me, k, a, step), q1s.at[p, r], q1r.at[p, r])

    def s5(r):
        for p in PARTS:
            lo, size = out_cols(p, r)
            cols = pl.ds(lo, size)
            wait(ra[p].at[:, :, cols], q1r.at[p, r])
            total = at(xs[p], (k,), (lo, size), me)[...].astype(F32)
            for j in range(3):
                total = total + ra[p][j, :, cols].astype(F32)
            col = p * W + lo - GATES
            span = slice(col, col + size)
            out_ref[:, span] = (mixed_ref[:, span].astype(F32) + total).astype(BF16)


    for p in PARTS:
        p1_start(p)
    for p in PARTS:
        p1_wait(p)
        for r in range(3):
            p2_start(p, r)
    p3_start(0)
    p3_start(1)
    p3_forward(0)
    p3_start(2)
    p3_finish(0)
    for load in loads:
        load.wait()
    twin_wait(0)
    selections()
    p3_forward(1)
    compact(0)
    gate_up(0)
    p3_finish(1)
    p3_forward(2)
    twin_wait(1)
    compact(1)
    gate_up(1)
    p3_finish(2)
    twin_wait(2)
    compact(2)
    gate_up(2)
    for p in PARTS:
        wait(xs[p].at[0, 0, 0, pl.ds(0, 3)], p1s.at[p])
        for r in range(3):
            cols = pl.ds(*AG_ROUNDS[r])
            wait(p2_bytes(p, r), p2s.at[p, r])
            wait(xs[p].at[0, pl.ds(0, 3), :, :, :, cols], p3s.at[p, r])
            wait(xs[p].at[0, :, :, :, :, cols], ds.at[p, r])
    down(0)
    s1(0)
    down(1)
    s2(0)
    s1(1)
    down(2)
    s2(1)
    s1(2)
    s3(0)
    s2(2)
    s4(0)
    s3(1)
    s5(0)
    s4(1)
    s3(2)
    s5(1)
    s4(2)
    s5(2)
    for p in PARTS:
        for r in range(3):
            cols = pl.ds(*out_cols(p, r))
            wait(xs[p].at[0, :, :, :, :, cols], qds.at[p, r])
            wait(rf[p].at[:, :, :, :, cols], qfs.at[p, r])
            wait(rr[p].at[:, :, :, :, cols], q3s.at[p, r])
            wait(rb[p].at[:, :, :, cols], q2s.at[p, r])
            wait(ra[p].at[:, :, cols], q1s.at[p, r])


def experts(rows, mixed, w_gate, w_up, w_down):
    vmem = pl.BlockSpec(memory_space=pltpu.VMEM)
    hbm = pl.BlockSpec(memory_space=pl.ANY)
    dma = pltpu.SemaphoreType.DMA

    def half_shape(p):
        a, b, c = ORDER[p]
        return (2, *[2 if axis == b else 4 for axis in "zyx" if axis != c], TOK, W)

    scratch = (
        [pltpu.VMEM((2, 4, 4, 4, TOK, W), BF16)] * 3
        + [pltpu.VMEM((4, 4, 4, TOK, W), BF16)] * 3
        + [pltpu.VMEM(half_shape(p), BF16) for p in PARTS]
        + [pltpu.VMEM((2, 4, 4, TOK, W), BF16)] * 3
        + [pltpu.VMEM((3, 4, TOK, W), BF16)] * 3
        + [pltpu.VMEM((3, TOK, W), BF16)] * 3
        + [
            pltpu.VMEM((2, D, 2 * FF), BF16),
            pltpu.VMEM((2, FF, D), BF16),
            pltpu.VMEM((2, 8 * SLOTS, 1536), BF16),
            pltpu.VMEM((2, 8 * SLOTS, 2 * FF), F32),
            pltpu.VMEM((2, 8 * SLOTS, FF), BF16),
            pltpu.VMEM((8, 2 * SLOTS, GROUP), BF16),
            pltpu.VMEM((8, GROUP, 2 * SLOTS), BF16),
            pltpu.VMEM((2, 8 * SLOTS, 128), F32),
        ]
        + [dma((5,)), dma((3,)), dma((3,)), dma((3, 3)), dma((3, 3)), dma((3, 3)), dma((3, 3, 3)), dma((3, 3)), dma((3, 3))]
        + [dma((3, 3)), dma((3, 3)), dma((3, 3)), dma((3, 3, 2))]
        + [dma((3, 3))] * 6
    )
    return pl.pallas_call(
        expert_kernel,
        out_shape=jax.ShapeDtypeStruct((TOK, D), BF16),
        in_specs=[vmem, vmem, hbm, hbm, hbm],
        out_specs=vmem,
        scratch_shapes=scratch,
        compiler_params=pltpu.CompilerParams(
            collective_id=1, has_side_effects=True, vmem_limit_bytes=VMEM
        ),
    )(rows, mixed, w_gate, w_up, w_down)


def on_device(
    query_rows,
    key_rows,
    value_rows,
    residual,
    out_proj,
    post_gain,
    router,
    routes,
    w_gate,
    w_up,
    w_down,
):
    rows, mixed = front(
        query_rows, key_rows, value_rows, residual, out_proj, post_gain, router, routes
    )
    return experts(rows, mixed, w_gate, w_up, w_down)[None]


def solution(mesh):
    in_specs = (
        P("dp", "ctx", "tensor"),
        P("dp", "ctx", None),
        P("dp", "ctx", None),
        P("dp", ("ctx", "tensor"), None),
        P("tensor", None),
        P(),
        P(),
        P("dp", ("ctx", "tensor"), None),
        P(("ctx", "tensor"), None, "dp"),
        P(("ctx", "tensor"), None, "dp"),
        P(("ctx", "tensor"), "dp", None),
    )
    out_specs = P("dp", ("ctx", "tensor"), None)
    return jax.shard_map(
        on_device, mesh=mesh, in_specs=in_specs, out_specs=out_specs, check_vma=False
    )
```

profile of v0, /device:TPU:0, one launch (start us, length us, event | category | flops | bytes accessed | tf_op | source)
XLA Modules:
  0.0 160.7 jit_solution(6192526497145964246)
XLA Ops:
  0.0 0.8 copy.15.routes_ref
  0.8 0.7 reshape.3.gain_ref
  1.5 1.5 copy.14.router_ref
  3.0 0.0 copy-start
  3.0 0.9 copy-done
  3.9 0.0 copy-start.1
  4.0 0.9 copy-done.1
  4.9 0.0 copy-start.4
  4.9 0.9 copy-done.4
  5.8 0.0 copy-start.5
  5.8 0.9 copy-done.5
  6.7 0.0 copy-start.6
  6.7 0.8 copy-done.6
  7.5 0.0 copy-start.7
  7.6 0.8 copy-done.7
  8.4 22.1 %shard_map.127 = (bf16[16,4224]{1,0:T(8,128)(2,1)S(1)}, bf16[16,4096]{1,0:T(8,128)(2,1)S(1)}) custom-call(bf16[1,128,512]{2,1,0:T(8,128)(2,1)S(1)} %copy-done.4, bf16[1,128,256]{2,1,0:T(8,128)(2,1)S(1)} %copy-done.6, bf16[1,128,256]{2,1,0:T(8,128)(2,1)S(1)} %copy-done.7, bf16[1,16,4096]{2,1,0:T(8,128)(2,1)S(1)} %copy-done.5, bf16[512,4096]{1,0:T(8,128)(2,1)} %proj_hbm.1, ...), custom_call_target="tpu_custom_call" | custom-call | tf_op jit(solution)/shard_map/pallas_call | solution.py:181
  30.5 0.0 copy-start.2
  30.5 0.6 copy-done.2
  31.2 0.0 copy-start.3
  31.2 0.7 copy-done.3
  31.8 127.3 %shard_map.128 = bf16[16,4096]{1,0:T(8,128)(2,1)} custom-call(bf16[16,4224]{1,0:T(8,128)(2,1)} %copy-done.2, bf16[16,4096]{1,0:T(8,128)(2,1)} %copy-done.3, bf16[2,4096,384]{2,1,0:T(8,128)(2,1)} %gate_hbm.1, bf16[2,4096,384]{2,1,0:T(8,128)(2,1)} %up_hbm.1, bf16[2,384,4096]{2,1,0:T(8,128)(2,1)} %down_hbm.1), custom_call_target="tpu_custom_call" | custom-call | tf_op jit(solution)/shard_map/pallas_call | solution.py:600
  159.1 1.6 copy.17
Async XLA Ops:
  3.0 1.0 copy-start
  3.9 0.9 copy-start.1
  4.9 0.9 copy-start.4
  5.8 0.9 copy-start.5
  6.7 0.8 copy-start.6
  7.5 0.8 copy-start.7
  30.5 0.7 copy-start.2
  31.2 0.7 copy-start.3
where the time goes:
time: 162 us; the launch traced here: 161 us
  Pallas kernels  149 us (92%)
  local copies, waits for them, and re-layouts  11.2 us (7%)
    pallas_call x1, Pallas kernels, experts(): pl.pallas_call(expert_kernel, out_shape=jax.ShapeDtypeStruct((TOK, D), BF...  127 us
    pallas_call x1, Pallas kernels, front(): pl.pallas_call(front_kernel, out_shape=(jax.ShapeDtypeStruct((TOK, WIDE),...  22.1 us
    unnamed x19, local copies, waits for them, and re-layouts  10.5 us

commit v1 on v0

--- a/solution.py
+++ b/solution.py
@@ -218,13 +218,43 @@
     me, k = place()
     twin = sibling(me, k)
 
-    loads = []
-    for e in range(2):
-        loads.append(pltpu.make_async_copy(gate_hbm.at[e], wgu.at[e, :, pl.ds(0, FF)], w_sem.at[e]))
-        loads.append(pltpu.make_async_copy(up_hbm.at[e], wgu.at[e, :, pl.ds(FF, FF)], w_sem.at[2 + e]))
-    loads.append(pltpu.make_async_copy(down_hbm, wd, w_sem.at[4]))
-    for load in loads:
-        load.start()
+    def spans(r):
+        found, at_col = [], 0
+        for p in PARTS:
+            lo, size = AG_ROUNDS[r]
+            if p == 0 and lo == 0:
+                lo, size = GATES, size - GATES
+            found.append((p, lo, size, at_col))
+            at_col += size
+        return found
+
+    def weights(r):
+        copies = []
+        for e in range(2):
+            for n, hbm in enumerate((gate_hbm, up_hbm)):
+                for p, lo, size, col in spans(r):
+                    from_row = p * W + lo - GATES
+                    copies.append(
+                        pltpu.make_async_copy(
+                            hbm.at[e, pl.ds(from_row, size), :],
+                            wgu.at[r % 2, e, pl.ds(col, size), pl.ds(n * FF, FF)],
+                            w_sem.at[r],
+                        )
+                    )
+        return copies
+
+    def weights_start(r):
+        for copy in weights(r):
+            copy.start()
+
+    def weights_wait(r):
+        total = sum(size for p, lo, size, col in spans(r))
+        wait(wgu.at[r % 2, :, pl.ds(0, total), :], w_sem.at[r])
+
+    load_down = pltpu.make_async_copy(down_hbm, wd, w_sem.at[3])
+    weights_start(0)
+    weights_start(1)
+    load_down.start()
     for p in PARTS:
         xs[p][k, me["z"], me["y"], me["x"]] = rows_ref[:, p * W : (p + 1) * W]
     greet(me, k, "xyz")
@@ -321,17 +351,7 @@
             unpick[g] = both.T.astype(BF16)
             return carry
 
-        lax.fori_loop(0, 8, one, 0)
-
-    def spans(r):
-        found, at_col = [], 0
-        for p in PARTS:
-            lo, size = AG_ROUNDS[r]
-            if p == 0 and lo == 0:
-                lo, size = GATES, size - GATES
-            found.append((p, lo, size, at_col))
-            at_col += size
-        return found
+        lax.fori_loop(0, 8, one, 0, unroll=True)
 
     def compact(r):
         for p, lo, size, col in spans(r):
@@ -342,18 +362,14 @@
                     packed[e, pl.ds(g * SLOTS, SLOTS), col : col + size] = rows[e * SLOTS : (e + 1) * SLOTS]
                 return carry
 
-            lax.fori_loop(0, 8, one, 0)
+            lax.fori_loop(0, 8, one, 0, unroll=True)
 
     def gate_up(r):
         def one(e, carry):
-            total = None
-            for p, lo, size, col in spans(r):
-                from_row = p * W + lo - GATES
-                term = jnp.dot(
-                    packed[e, :, col : col + size], wgu[e, from_row : from_row + size, :],
-                    preferred_element_type=F32,
-                )
-                total = term if total is None else total + term
+            depth = sum(size for p, lo, size, col in spans(r))
+            total = jnp.dot(
+                packed[e, :, :depth], wgu[r % 2, e, :depth, :], preferred_element_type=F32
+            )
             if r > 0:
                 total = total + acc[e]
             if r < len(AG_ROUNDS) - 1:
@@ -363,7 +379,7 @@
                 hidden[e] = (gate / (1.0 + jnp.exp(-gate)) * up).astype(BF16)
             return carry
 
-        lax.fori_loop(0, 2, one, 0)
+        lax.fori_loop(0, 2, one, 0, unroll=True)
 
 
     def out_cols(p, r):
@@ -382,7 +398,7 @@
                 packed[e, :, :size] = (part * row_gate[e, :, 0:1]).astype(BF16)
                 return carry
 
-            lax.fori_loop(0, 2, product, 0)
+            lax.fori_loop(0, 2, product, 0, unroll=True)
 
             def one(i, carry, p=p, lo=lo, size=size):
                 g = (i + 4 * (1 - k)) % 8
@@ -393,10 +409,10 @@
                 xs[p][g // 4, g % 4, :, :, :, lo : lo + size] = tokens.reshape(4, 4, TOK, size)
                 return carry
 
-            lax.fori_loop(0, 4, one, 0)
+            lax.fori_loop(0, 4, one, 0, unroll=True)
             cols = (lo, size)
             send(at(xs[p], (1 - k,), cols, {}), at(rd[p], (), cols, {}), twin, qds.at[p, r], qdr.at[p, r])
-            lax.fori_loop(4, 8, one, 0)
+            lax.fori_loop(4, 8, one, 0, unroll=True)
 
     def total_into(dst, refs):
         total = refs[0][...].astype(F32)
@@ -419,7 +435,7 @@
             total_into(mine, [mine, unit_of(rd[p], (), p, r, step, 4, i)])
             return carry
 
-        lax.fori_loop(0, 4, one, 0)
+        lax.fori_loop(0, 4, one, 0, unroll=True)
 
     def piece_of(ref, lead, p, r, fix):
         a, b, c = ORDER[p]
@@ -459,7 +475,7 @@
                     total_into(mine, [mine, half_slot(p, r, half, i)])
                     return carry
 
-                lax.fori_loop(0, 2, one, 0)
+                lax.fori_loop(0, 2, one, 0, unroll=True)
                 src = unit_of(xs[p], (k,), p, r, way)
                 slot = piece_of(rr[p], (half,), p, r, {})
                 send(src, slot, device(me, k, c, way), q3s.at[p, r], q3r.at[p, r])
@@ -475,7 +491,7 @@
                 total_into(mine, [mine] + [piece_of(rr[p], (h,), p, r, {b: i}) for h in range(2)])
                 return carry
 
-            lax.fori_loop(0, 4, one, 0)
+            lax.fori_loop(0, 4, one, 0, unroll=True)
             for step in (2, 1, 3):
                 src = unit_of(xs[p], (k,), p, r, 0, 4, (me[b] + step) % 4)
                 slot = rb[p].at[step - 1, :, :, pl.ds(*out_cols(p, r))]
@@ -516,22 +532,25 @@
     p3_forward(0)
     p3_start(2)
     p3_finish(0)
-    for load in loads:
-        load.wait()
     twin_wait(0)
     selections()
     p3_forward(1)
     compact(0)
+    weights_wait(0)
     gate_up(0)
+    weights_start(2)
     p3_finish(1)
     p3_forward(2)
     twin_wait(1)
     compact(1)
+    weights_wait(1)
     gate_up(1)
     p3_finish(2)
     twin_wait(2)
     compact(2)
+    weights_wait(2)
     gate_up(2)
+    load_down.wait()
     for p in PARTS:
         wait(xs[p].at[0, 0, 0, pl.ds(0, 3)], p1s.at[p])
         for r in range(3):
@@ -584,7 +603,7 @@
         + [pltpu.VMEM((3, 4, TOK, W), BF16)] * 3
         + [pltpu.VMEM((3, TOK, W), BF16)] * 3
         + [
-            pltpu.VMEM((2, D, 2 * FF), BF16),
+            pltpu.VMEM((2, 2, 1536, 2 * FF), BF16),
             pltpu.VMEM((2, FF, D), BF16),
             pltpu.VMEM((2, 8 * SLOTS, 1536), BF16),
             pltpu.VMEM((2, 8 * SLOTS, 2 * FF), F32),
@@ -593,7 +612,7 @@
             pltpu.VMEM((8, GROUP, 2 * SLOTS), BF16),
             pltpu.VMEM((2, 8 * SLOTS, 128), F32),
         ]
-        + [dma((5,)), dma((3,)), dma((3,)), dma((3, 3)), dma((3, 3)), dma((3, 3)), dma((3, 3, 3)), dma((3, 3)), dma((3, 3))]
+        + [dma((4,)), dma((3,)), dma((3,)), dma((3, 3)), dma((3, 3)), dma((3, 3)), dma((3, 3, 3)), dma((3, 3)), dma((3, 3))]
         + [dma((3, 3)), dma((3, 3)), dma((3, 3)), dma((3, 3, 2))]
         + [dma((3, 3))] * 6
     )

time: 162 us -> 139 us (0.86)
  Pallas kernels: 149 us -> 127 us
    pallas_call x1, Pallas kernels: 127 us -> 105 us  [experts(): pl.pallas_call(expert_kernel, out_shape=jax.ShapeDtypeStruct((TOK, D), BF...]
where the time goes in v1:
time: 139 us; the launch traced here: 138 us
  Pallas kernels  127 us (91%)
  local copies, waits for them, and re-layouts  11.2 us (8%)
    pallas_call x1, Pallas kernels, experts(): pl.pallas_call(expert_kernel, out_shape=jax.ShapeDtypeStruct((TOK, D), BF...  105 us
    pallas_call x1, Pallas kernels, front(): pl.pallas_call(front_kernel, out_shape=(jax.ShapeDtypeStruct((TOK, WIDE),...  22.1 us
    unnamed x19, local copies, waits for them, and re-layouts  10.5 us

profile of v1, /device:TPU:0, one launch (start us, length us, event | category | flops | bytes accessed | tf_op | source)
XLA Modules:
  0.0 138.5 jit_solution(824444807482856818)
XLA Ops:
  0.0 0.8 copy.15.routes_ref
  0.8 0.7 reshape.3.gain_ref
  1.5 1.5 %copy.14.router_ref = bf16[4096,64]{1,0:T(8,128)(2,1)S(1)} copy(bf16[4096,64]{0,1:T(8,128)(2,1)} %param.19) | data formatting | bytes 1048576 | tf_op args[6]
  3.0 0.0 copy-start
  3.0 0.9 copy-done
  3.9 0.0 copy-start.1
  4.0 0.9 copy-done.1
  4.9 0.0 copy-start.4
  4.9 0.9 copy-done.4
  5.8 0.0 copy-start.5
  5.8 0.9 copy-done.5
  6.7 0.0 copy-start.6
  6.7 0.8 copy-done.6
  7.5 0.0 copy-start.7
  7.6 0.8 copy-done.7
  8.4 22.1 %shard_map.127 = (bf16[16,4224]{1,0:T(8,128)(2,1)S(1)}, bf16[16,4096]{1,0:T(8,128)(2,1)S(1)}) custom-call(bf16[1,128,512]{2,1,0:T(8,128)(2,1)S(1)} %copy-done.4, bf16[1,128,256]{2,1,0:T(8,128)(2,1)S(1)} %copy-done.6, bf16[1,128,256]{2,1,0:T(8,128)(2,1)S(1)} %copy-done.7, bf16[1,16,4096]{2,1,0:T(8,128)(2,1)S(1)} %copy-done.5, bf16[512,4096]{1,0:T(8,128)(2,1)} %proj_hbm.1, ...), custom_call_target="tpu_custom_call" | custom-call | tf_op jit(solution)/shard_map/pallas_call | solution.py:181
  30.5 0.0 copy-start.2
  30.5 0.6 copy-done.2
  31.2 0.0 copy-start.3
  31.2 0.7 copy-done.3
  31.8 105.1 %shard_map.128 = bf16[16,4096]{1,0:T(8,128)(2,1)} custom-call(bf16[16,4224]{1,0:T(8,128)(2,1)} %copy-done.2, bf16[16,4096]{1,0:T(8,128)(2,1)} %copy-done.3, bf16[2,4096,384]{2,1,0:T(8,128)(2,1)} %gate_hbm.1, bf16[2,4096,384]{2,1,0:T(8,128)(2,1)} %up_hbm.1, bf16[2,384,4096]{2,1,0:T(8,128)(2,1)} %down_hbm.1), custom_call_target="tpu_custom_call" | custom-call | tf_op jit(solution)/shard_map/pallas_call | solution.py:619
  136.9 1.6 %copy.17 = bf16[1,16,4096]{2,1,0:T(8,128)(2,1)} copy(bf16[1,16,4096]{2,1,0:T(8,128)(2,1)} %bitcast.1) | data formatting | bytes 262144
Async XLA Ops:
  3.0 1.0 copy-start
  3.9 0.9 copy-start.1
  4.9 0.9 copy-start.4
  5.8 0.9 copy-start.5
  6.7 0.8 copy-start.6
  7.5 0.8 copy-start.7
  30.5 0.7 copy-start.2
  31.2 0.7 copy-start.3

commit v2 on v1

--- a/solution.py
+++ b/solution.py
@@ -1,5 +1,3 @@
-import functools
-
 import jax
 import jax.numpy as jnp
 import numpy as np
@@ -95,31 +93,98 @@
     return (values * cosine + pltpu.roll(values, HEAD // 2, 1) * sine).astype(BF16)
 
 
-def front_kernel(
-    query_ref, key_ref, value_ref, residual_ref, proj_hbm, gain_ref, router_ref, routes_ref,
-    cos_ref, sin_ref, rows_ref, mixed_ref,
-    proj, kv, qrot, krot, partial, far, from_sibling, from_ring,
-    proj_sem, kv_send, kv_recv, sib_send, sib_recv, ring_send, ring_recv,
+def layer_kernel(
+    query_hbm, key_hbm, value_hbm, residual_hbm, proj_hbm, gain_hbm, router_hbm, routes_hbm,
+    cos_hbm, sin_hbm, gate_hbm, up_hbm, down_hbm, out_ref,
+    query, residual, gain, router, routes, cosine, sine,
+    kv, qrot, krot, far, from_sibling, from_ring, mixed,
+    x0, x1, x2, rd0, rd1, rd2, rf0, rf1, rf2, rr0, rr1, rr2, rb0, rb1, rb2, ra0, ra1, ra2,
+    wgu, wd, packed, acc, hidden, pick, unpick, row_gate,
+    in_sem, kv_send, kv_recv, sib_send, sib_recv, ring_send, ring_recv,
+    w_sem, p1s, p1r, p2s, p2r, p3s, p3r, ds, dr,
+    qds, qdr, qfs, qfr, q3s, q3r, q2s, q2r, q1s, q1r,
 ):
+    xs, rd, rf, rr = (x0, x1, x2), (rd0, rd1, rd2), (rf0, rf1, rf2), (rr0, rr1, rr2)
+    rb, ra = (rb0, rb1, rb2), (ra0, ra1, ra2)
     me, k = place()
-    t = lax.axis_index("tensor")
+    twin = sibling(me, k)
+
+    def spans(r):
+        found, at_col = [], 0
+        for p in PARTS:
+            lo, size = AG_ROUNDS[r]
+            if p == 0 and lo == 0:
+                lo, size = GATES, size - GATES
+            found.append((p, lo, size, at_col))
+            at_col += size
+        return found
+
+    def weights(r):
+        copies = []
+        for e in range(2):
+            for n, hbm in enumerate((gate_hbm, up_hbm)):
+                for p, lo, size, col in spans(r):
+                    from_row = p * W + lo - GATES
+                    copies.append(
+                        pltpu.make_async_copy(
+                            hbm.at[e, pl.ds(from_row, size), :],
+                            wgu.at[r % 2, e, pl.ds(col, size), pl.ds(n * FF, FF)],
+                            w_sem.at[r],
+                        )
+                    )
+        return copies
+
+    def weights_start(r):
+        for copy in weights(r):
+            copy.start()
+
+    def weights_wait(r):
+        total = sum(size for p, lo, size, col in spans(r))
+        wait(wgu.at[r % 2, :, pl.ds(0, total), :], w_sem.at[r])
+
+    load_down = pltpu.make_async_copy(down_hbm, wd, w_sem.at[3])
+
+
+    head = pl.multiple_of((lax.axis_index("tensor") // 4) * HEAD, HEAD)
     y = me["y"]
-    load = pltpu.make_async_copy(proj_hbm, proj, proj_sem)
-    load.start()
-    head = pl.multiple_of((t // 4) * HEAD, HEAD)
-    kv[y, 0] = key_ref[0, :, pl.ds(head, HEAD)]
-    kv[y, 1] = value_ref[0, :, pl.ds(head, HEAD)]
-    greet(me, k, "xy")
-    for step in (1, 2, 3):
+    loads = [
+        pltpu.make_async_copy(src, dst, in_sem.at[i])
+        for i, (src, dst) in enumerate(
+            (
+                (key_hbm.at[0, :, pl.ds(head, HEAD)], kv.at[y, 0]),
+                (value_hbm.at[0, :, pl.ds(head, HEAD)], kv.at[y, 1]),
+                (query_hbm.at[0], query),
+                (cos_hbm, cosine),
+                (sin_hbm, sine),
+                (proj_hbm.at[pl.ds(0, FF)], wd.at[0]),
+                (proj_hbm.at[pl.ds(FF, HEADS * HEAD - FF)], wd.at[1, pl.ds(0, HEADS * HEAD - FF)]),
+                (residual_hbm.at[0], residual),
+                (gain_hbm, gain),
+                (router_hbm, router),
+                (routes_hbm.at[0], routes),
+            )
+        )
+    ]
+    for load in loads:
+        load.start()
+    weights_start(0)
+    weights_start(1)
+    greet(me, k, "xyz")
+    for load in loads[:2]:
+        load.wait()
+    for step in (2, 1, 3):
         send(kv.at[y], kv.at[y], device(me, k, "y", step), kv_send, kv_recv)
+    for load in loads[2:5]:
+        load.wait()
     own = pl.ds(pl.multiple_of(y * LOCAL, LOCAL), LOCAL)
-    cosine, sine = cos_ref[own, :], sin_ref[own, :]
     for h in range(HEADS):
-        qrot[pl.ds(h * LOCAL, LOCAL), :] = turn(query_ref[0, :, h * HEAD : (h + 1) * HEAD], cosine, sine)
+        qrot[pl.ds(h * LOCAL, LOCAL), :] = turn(
+            query[:, h * HEAD : (h + 1) * HEAD], cosine[own, :], sine[own, :]
+        )
     wait(kv.at[pl.ds(0, 3)], kv_recv)
     for c in range(4):
         span = pl.ds(c * LOCAL, LOCAL)
-        krot[span, :] = turn(kv[c, 0], cos_ref[span, :], sin_ref[span, :])
+        krot[span, :] = turn(kv[c, 0], cosine[span, :], sine[span, :])
     values = kv[:, 1].reshape(SEQ, HEAD)
     place_q = y * LOCAL + lax.broadcasted_iota(jnp.int32, (LOCAL, SEQ), 0)
     causal = place_q >= lax.broadcasted_iota(jnp.int32, (LOCAL, SEQ), 1)
@@ -136,129 +201,59 @@
         summed = jnp.dot(expon.astype(BF16), values, preferred_element_type=F32)
         attended.append((summed / total).astype(BF16))
     attended = jnp.concatenate(attended, axis=1)
-    load.wait()
+    for load in loads[5:]:
+        load.wait()
     for c in range(8):
         cols = slice(c * 512, (c + 1) * 512)
-        out = jnp.dot(attended, proj[:, cols], preferred_element_type=F32)
-        partial[:, :, :, cols] = out.reshape(4, 2, TOK, 512)
-        far[:, :, cols] = partial[:, 1 - k, :, cols].astype(BF16)
-    to = sibling(me, k)
-    send(far, from_sibling, to, sib_send, sib_recv)
-    wait(far, sib_send)
-    wait(from_sibling, sib_recv)
-    for step in (2, 1, 3):
-        v = (me["x"] + step) % 4
-        far[v] = (partial[v, k] + from_sibling[v].astype(F32)).astype(BF16)
-        send(far.at[v], from_ring.at[step - 1], device(me, k, "x", step), ring_send, ring_recv)
-    own_sum = partial[me["x"], k] + from_sibling[me["x"]].astype(F32)
-    wait(from_ring, ring_recv)
-    projected = own_sum + from_ring[0].astype(F32) + from_ring[1].astype(F32) + from_ring[2].astype(F32)
-    mixed = (residual_ref[0].astype(F32) + projected).astype(BF16)
-    mixed_ref[...] = mixed
-    wide = mixed.astype(F32)
-    scale = lax.rsqrt(jnp.mean(wide * wide, axis=-1, keepdims=True) + 1e-06)
-    normed = (wide * scale * gain_ref[...].astype(F32)).astype(BF16)
-    rows_ref[:, GATES:] = normed
-    logits = jnp.dot(normed, router_ref[...], preferred_element_type=F32)
-    lane = lax.broadcasted_iota(jnp.int32, (TOK, EXPERTS), 1)
-    routes = routes_ref[0]
-    chosen = routes[:, 0:1] == lane
-    for j in range(1, 8):
-        chosen = jnp.logical_or(chosen, routes[:, j : j + 1] == lane)
-    peak = jnp.max(jnp.where(chosen, logits, F32(-3e38)), axis=-1, keepdims=True)
-    expon = jnp.where(chosen, jnp.exp(logits - peak), F32(0.0))
-    gates = expon / jnp.sum(expon, axis=-1, keepdims=True)
-    high = gates.astype(BF16).astype(F32)
-    rows_ref[:, :GATES] = jnp.concatenate([high, gates - high], axis=1).astype(BF16)
-    wait(kv.at[pl.ds(0, 3)], kv_send)
-    wait(from_ring, ring_send)
-
-
-def front(query_rows, key_rows, value_rows, residual, out_proj, post_gain, router, routes):
-    cosine, sine = rope_tables()
-    vmem = pl.BlockSpec(memory_space=pltpu.VMEM)
-    dma = pltpu.SemaphoreType.DMA
-    return pl.pallas_call(
-        front_kernel,
-        out_shape=(
-            jax.ShapeDtypeStruct((TOK, WIDE), BF16),
-            jax.ShapeDtypeStruct((TOK, D), BF16),
-        ),
-        in_specs=[vmem] * 4 + [pl.BlockSpec(memory_space=pl.ANY)] + [vmem] * 5,
-        out_specs=(vmem, vmem),
-        scratch_shapes=[
-            pltpu.VMEM((HEADS * HEAD, D), BF16),
-            pltpu.VMEM((4, 2, LOCAL, HEAD), BF16),
-            pltpu.VMEM((HEADS * LOCAL, HEAD), BF16),
-            pltpu.VMEM((SEQ, HEAD), BF16),
-            pltpu.VMEM((4, 2, TOK, D), F32),
-            pltpu.VMEM((4, TOK, D), BF16),
-            pltpu.VMEM((4, TOK, D), BF16),
-            pltpu.VMEM((3, TOK, D), BF16),
-            dma, dma, dma, dma, dma, dma, dma,
-        ],
-        compiler_params=pltpu.CompilerParams(
-            collective_id=0, has_side_effects=True, vmem_limit_bytes=48 * 2**20
-        ),
-    )(
-        query_rows, key_rows, value_rows, residual, out_proj, post_gain.reshape(1, D), router, routes,
-        jnp.asarray(cosine), jnp.asarray(sine),
-    )
-
-
-def expert_kernel(
-    rows_ref, mixed_ref, gate_hbm, up_hbm, down_hbm, out_ref,
-    x0, x1, x2, rd0, rd1, rd2, rf0, rf1, rf2, rr0, rr1, rr2, rb0, rb1, rb2, ra0, ra1, ra2,
-    wgu, wd, packed, acc, hidden, pick, unpick, row_gate,
-    w_sem, p1s, p1r, p2s, p2r, p3s, p3r, ds, dr,
-    qds, qdr, qfs, qfr, q3s, q3r, q2s, q2r, q1s, q1r,
-):
-    xs, rd, rf, rr = (x0, x1, x2), (rd0, rd1, rd2), (rf0, rf1, rf2), (rr0, rr1, rr2)
-    rb, ra = (rb0, rb1, rb2), (ra0, ra1, ra2)
-    me, k = place()
-    twin = sibling(me, k)
-
-    def spans(r):
-        found, at_col = [], 0
-        for p in PARTS:
-            lo, size = AG_ROUNDS[r]
-            if p == 0 and lo == 0:
-                lo, size = GATES, size - GATES
-            found.append((p, lo, size, at_col))
-            at_col += size
-        return found
-
-    def weights(r):
-        copies = []
-        for e in range(2):
-            for n, hbm in enumerate((gate_hbm, up_hbm)):
-                for p, lo, size, col in spans(r):
-                    from_row = p * W + lo - GATES
-                    copies.append(
-                        pltpu.make_async_copy(
-                            hbm.at[e, pl.ds(from_row, size), :],
-                            wgu.at[r % 2, e, pl.ds(col, size), pl.ds(n * FF, FF)],
-                            w_sem.at[r],
-                        )
-                    )
-        return copies
-
-    def weights_start(r):
-        for copy in weights(r):
-            copy.start()
-
-    def weights_wait(r):
-        total = sum(size for p, lo, size, col in spans(r))
-        wait(wgu.at[r % 2, :, pl.ds(0, total), :], w_sem.at[r])
-
-    load_down = pltpu.make_async_copy(down_hbm, wd, w_sem.at[3])
-    weights_start(0)
-    weights_start(1)
+        out = jnp.dot(attended[:, :FF], wd[0, :, cols], preferred_element_type=F32) + jnp.dot(
+            attended[:, FF:], wd[1, : HEADS * HEAD - FF, cols], preferred_element_type=F32
+        )
+        acc[c // 4, pl.ds((c % 4) * LOCAL, LOCAL), :512] = out
+        for v in range(4):
+            rows = pl.ds(pl.multiple_of((c % 4) * LOCAL + (2 * v + 1 - k) * TOK, TOK), TOK)
+            far[v, :, cols] = acc[c // 4, rows, :512].astype(BF16)
+        if c % 4 == 3:
+            half = pl.ds((c // 4) * 2048, 2048)
+            send(
+                far.at[:, :, half], from_sibling.at[:, :, half], twin,
+                sib_send.at[c // 4], sib_recv.at[c // 4],
+            )
     load_down.start()
-    for p in PARTS:
-        xs[p][k, me["z"], me["y"], me["x"]] = rows_ref[:, p * W : (p + 1) * W]
-    greet(me, k, "xyz")
-
+
+    def chip_sum(v, c):
+        rows = pl.ds(pl.multiple_of((c % 4) * LOCAL + (2 * v + k) * TOK, TOK), TOK)
+        return acc[c // 4, rows, :512] + from_sibling[v, :, c * 512 : (c + 1) * 512].astype(F32)
+
+    for i in range(2):
+        half = pl.ds(i * 2048, 2048)
+        wait(far.at[:, :, half], sib_send.at[i])
+        wait(from_sibling.at[:, :, half], sib_recv.at[i])
+        for step in (2, 1, 3):
+            v = (me["x"] + step) % 4
+            for c in range(4 * i, 4 * i + 4):
+                far[v, :, c * 512 : (c + 1) * 512] = chip_sum(v, c).astype(BF16)
+            send(
+                far.at[v, :, half], from_ring.at[step - 1, :, half], device(me, k, "x", step),
+                ring_send.at[i], ring_recv.at[i],
+            )
+    square = jnp.zeros((TOK, 1), F32)
+    for c in range(8):
+        cols = slice(c * 512, (c + 1) * 512)
+        if c % 4 == 0:
+            wait(from_ring.at[:, :, pl.ds((c // 4) * 2048, 2048)], ring_recv.at[c // 4])
+        projected = chip_sum(me["x"], c)
+        for j in range(3):
+            projected = projected + from_ring[j, :, cols].astype(F32)
+        wide = (residual[:, cols].astype(F32) + projected).astype(BF16)
+        mixed[:, cols] = wide
+        wide = wide.astype(F32)
+        square = square + jnp.sum(wide * wide, axis=-1, keepdims=True)
+    scale = lax.rsqrt(square / D + 1e-06)
+    for c in range(D // 128):
+        wide = mixed[:, c * 128 : (c + 1) * 128].astype(F32)
+        normed = (wide * scale * gain[c : c + 1, :].astype(F32)).astype(BF16)
+        col = GATES + c * 128
+        xs[col // W][k, me["z"], me["y"], me["x"], :, col % W : col % W + 128] = normed
     def at(ref, lead, cols, fix):
         index = [fix.get(axis, slice(None)) for axis in "zyx"]
         return ref.at[(*lead, *index, slice(None), pl.ds(*cols))]
@@ -322,6 +317,33 @@
     def twin_wait(r):
         for p in PARTS:
             wait(xs[p].at[1 - k, :, :, :, :, pl.ds(*AG_ROUNDS[r])], dr.at[p, r])
+
+    def gates():
+        logits = jnp.zeros((EXPERTS, TOK), F32)
+        for p in PARTS:
+            lo = GATES if p == 0 else 0
+            col = p * W + lo - GATES
+            normed = xs[p][k, me["z"], me["y"], me["x"], :, lo:W]
+            logits = logits + lax.dot_general(
+                router[:, col : col + W - lo], normed, (((1,), (1,)), ((), ())),
+                preferred_element_type=F32,
+            )
+        expert = lax.broadcasted_iota(jnp.int32, (EXPERTS, TOK), 0)
+        chosen = expert == routes[0:1, :]
+        for j in range(1, 8):
+            chosen = jnp.logical_or(chosen, expert == routes[j : j + 1, :])
+        peak = jnp.max(jnp.where(chosen, logits, F32(-3e38)), axis=0, keepdims=True)
+        expon = jnp.where(chosen, jnp.exp(logits - peak), F32(0.0))
+        gate = expon / jnp.sum(expon, axis=0, keepdims=True)
+        high = gate.astype(BF16).astype(F32)
+        both = jnp.concatenate([high, gate - high], axis=0).astype(BF16)
+        unit = lax.broadcasted_iota(jnp.int32, (TOK, TOK), 0) == lax.broadcasted_iota(
+            jnp.int32, (TOK, TOK), 1
+        )
+        turned = lax.dot_general(
+            unit.astype(F32).astype(BF16), both, (((1,), (1,)), ((), ())), preferred_element_type=F32
+        )
+        x0[k, me["z"], me["y"], me["x"], :, :GATES] = turned.astype(BF16)
 
 
     def selections():
@@ -518,12 +540,14 @@
                 total = total + ra[p][j, :, cols].astype(F32)
             col = p * W + lo - GATES
             span = slice(col, col + size)
-            out_ref[:, span] = (mixed_ref[:, span].astype(F32) + total).astype(BF16)
-
-
-    for p in PARTS:
-        p1_start(p)
-    for p in PARTS:
+            out_ref[:, span] = (mixed[:, span].astype(F32) + total).astype(BF16)
+
+
+    p1_start(1)
+    p1_start(2)
+    gates()
+    p1_start(0)
+    for p in (1, 2, 0):
         p1_wait(p)
         for r in range(3):
             p2_start(p, r)
@@ -559,13 +583,13 @@
             wait(xs[p].at[0, pl.ds(0, 3), :, :, :, cols], p3s.at[p, r])
             wait(xs[p].at[0, :, :, :, :, cols], ds.at[p, r])
     down(0)
+    down(1)
     s1(0)
-    down(1)
+    down(2)
+    s1(1)
     s2(0)
-    s1(1)
-    down(2)
+    s1(2)
     s2(1)
-    s1(2)
     s3(0)
     s2(2)
     s4(0)
@@ -576,6 +600,9 @@
     s5(1)
     s4(2)
     s5(2)
+    wait(kv.at[pl.ds(0, 3)], kv_send)
+    for i in range(2):
+        wait(from_ring.at[:, :, pl.ds(i * 2048, 2048)], ring_send.at[i])
     for p in PARTS:
         for r in range(3):
             cols = pl.ds(*out_cols(p, r))
@@ -584,48 +611,6 @@
             wait(rr[p].at[:, :, :, :, cols], q3s.at[p, r])
             wait(rb[p].at[:, :, :, cols], q2s.at[p, r])
             wait(ra[p].at[:, :, cols], q1s.at[p, r])
-
-
-def experts(rows, mixed, w_gate, w_up, w_down):
-    vmem = pl.BlockSpec(memory_space=pltpu.VMEM)
-    hbm = pl.BlockSpec(memory_space=pl.ANY)
-    dma = pltpu.SemaphoreType.DMA
-
-    def half_shape(p):
-        a, b, c = ORDER[p]
-        return (2, *[2 if axis == b else 4 for axis in "zyx" if axis != c], TOK, W)
-
-    scratch = (
-        [pltpu.VMEM((2, 4, 4, 4, TOK, W), BF16)] * 3
-        + [pltpu.VMEM((4, 4, 4, TOK, W), BF16)] * 3
-        + [pltpu.VMEM(half_shape(p), BF16) for p in PARTS]
-        + [pltpu.VMEM((2, 4, 4, TOK, W), BF16)] * 3
-        + [pltpu.VMEM((3, 4, TOK, W), BF16)] * 3
-        + [pltpu.VMEM((3, TOK, W), BF16)] * 3
-        + [
-            pltpu.VMEM((2, 2, 1536, 2 * FF), BF16),
-            pltpu.VMEM((2, FF, D), BF16),
-            pltpu.VMEM((2, 8 * SLOTS, 1536), BF16),
-            pltpu.VMEM((2, 8 * SLOTS, 2 * FF), F32),
-            pltpu.VMEM((2, 8 * SLOTS, FF), BF16),
-            pltpu.VMEM((8, 2 * SLOTS, GROUP), BF16),
-            pltpu.VMEM((8, GROUP, 2 * SLOTS), BF16),
-            pltpu.VMEM((2, 8 * SLOTS, 128), F32),
-        ]
-        + [dma((4,)), dma((3,)), dma((3,)), dma((3, 3)), dma((3, 3)), dma((3, 3)), dma((3, 3, 3)), dma((3, 3)), dma((3, 3))]
-        + [dma((3, 3)), dma((3, 3)), dma((3, 3)), dma((3, 3, 2))]
-        + [dma((3, 3))] * 6
-    )
-    return pl.pallas_call(
-        expert_kernel,
-        out_shape=jax.ShapeDtypeStruct((TOK, D), BF16),
-        in_specs=[vmem, vmem, hbm, hbm, hbm],
-        out_specs=vmem,
-        scratch_shapes=scratch,
-        compiler_params=pltpu.CompilerParams(
-            collective_id=1, has_side_effects=True, vmem_limit_bytes=VMEM
-        ),
-    )(rows, mixed, w_gate, w_up, w_down)
 
 
 def on_device(
@@ -641,10 +626,69 @@
     w_up,
     w_down,
 ):
-    rows, mixed = front(
-        query_rows, key_rows, value_rows, residual, out_proj, post_gain, router, routes
+    vmem = pltpu.VMEM
+    hbm = pl.BlockSpec(memory_space=pl.ANY)
+    dma = pltpu.SemaphoreType.DMA
+    cosine, sine = rope_tables()
+
+    def half_shape(p):
+        a, b, c = ORDER[p]
+        return (2, *[2 if axis == b else 4 for axis in "zyx" if axis != c], TOK, W)
+
+    scratch = (
+        [
+            vmem((LOCAL, HEADS * HEAD), BF16),
+            vmem((TOK, D), BF16),
+            vmem((D // 128, 128), BF16),
+            vmem((EXPERTS, D), BF16),
+            vmem((8, TOK), jnp.int32),
+            vmem((SEQ, HEAD), F32),
+            vmem((SEQ, HEAD), F32),
+            vmem((4, 2, LOCAL, HEAD), BF16),
+            vmem((HEADS * LOCAL, HEAD), BF16),
+            vmem((SEQ, HEAD), BF16),
+            vmem((4, TOK, D), BF16),
+            vmem((4, TOK, D), BF16),
+            vmem((3, TOK, D), BF16),
+            vmem((TOK, D), BF16),
+        ]
+        + [vmem((2, 4, 4, 4, TOK, W), BF16)] * 3
+        + [vmem((4, 4, 4, TOK, W), BF16)] * 3
+        + [vmem(half_shape(p), BF16) for p in PARTS]
+        + [vmem((2, 4, 4, TOK, W), BF16)] * 3
+        + [vmem((3, 4, TOK, W), BF16)] * 3
+        + [vmem((3, TOK, W), BF16)] * 3
+        + [
+            vmem((2, 2, 1536, 2 * FF), BF16),
+            vmem((2, FF, D), BF16),
+            vmem((2, 8 * SLOTS, 1536), BF16),
+            vmem((2, 8 * SLOTS, 2 * FF), F32),
+            vmem((2, 8 * SLOTS, FF), BF16),
+            vmem((8, 2 * SLOTS, GROUP), BF16),
+            vmem((8, GROUP, 2 * SLOTS), BF16),
+            vmem((2, 8 * SLOTS, 128), F32),
+        ]
+        + [dma((11,)), dma, dma, dma((2,)), dma((2,)), dma((2,)), dma((2,))]
+        + [dma((4,)), dma((3,)), dma((3,)), dma((3, 3)), dma((3, 3)), dma((3, 3)), dma((3, 3, 3))]
+        + [dma((3, 3)), dma((3, 3))]
+        + [dma((3, 3)), dma((3, 3)), dma((3, 3)), dma((3, 3, 2))]
+        + [dma((3, 3))] * 6
     )
-    return experts(rows, mixed, w_gate, w_up, w_down)[None]
+    out = pl.pallas_call(
+        layer_kernel,
+        out_shape=jax.ShapeDtypeStruct((TOK, D), BF16),
+        in_specs=[hbm] * 13,
+        out_specs=pl.BlockSpec(memory_space=pltpu.VMEM),
+        scratch_shapes=scratch,
+        compiler_params=pltpu.CompilerParams(
+            collective_id=0, has_side_effects=True, vmem_limit_bytes=VMEM
+        ),
+    )(
+        query_rows, key_rows, value_rows, residual, out_proj, post_gain.reshape(D // 128, 128),
+        router.T, jnp.swapaxes(routes, 1, 2), jnp.asarray(cosine), jnp.asarray(sine),
+        w_gate, w_up, w_down,
+    )
+    return out[None]
 
 
 def solution(mesh):

time: 139 us -> 125 us (0.90)
  local copies, waits for them, and re-layouts: 11.2 us -> 1.57 us
  Pallas kernels: 127 us -> 123 us
    unnamed x19 -> x1, local copies, waits for them, and re-layouts: 10.5 us -> 1.57 us
    pallas_call x2 -> x1, Pallas kernels: 127 us -> 123 us  [on_device(): pl.pallas_call(layer_kernel, out_shape=jax.ShapeDtypeStruct((TOK, D), BF1...]
where the time goes in v2:
time: 125 us
  Pallas kernels  123 us (98%)
  local copies, waits for them, and re-layouts  1.57 us (1%)
    pallas_call x1, Pallas kernels, on_device(): pl.pallas_call(layer_kernel, out_shape=jax.ShapeDtypeStruct((TOK, D), BF1...  123 us

profile of v2, /device:TPU:0, one launch (start us, length us, event | category | flops | bytes accessed | tf_op | source)
XLA Modules:
  0.0 124.9 jit_solution(10215369481453727647)
XLA Ops:
  0.0 123.4 %shard_map.127 = bf16[16,4096]{1,0:T(8,128)(2,1)} custom-call(bf16[1,128,512]{2,1,0:T(8,128)(2,1)} %query_hbm.1, bf16[1,128,256]{2,1,0:T(8,128)(2,1)} %key_hbm.1, bf16[1,128,256]{2,1,0:T(8,128)(2,1)} %value_hbm.1, bf16[1,16,4096]{2,1,0:T(8,128)(2,1)} %residual_hbm.1, bf16[512,4096]{1,0:T(8,128)(2,1)} %proj_hbm.1, bf16[32,128]{1,0:T(8,128)(2,1)} %bitcast.6, ...), custom_call_target="tpu_custom_call" | custom-call | tf_op jit(solution)/shard_map/pallas_call | solution.py:677
  123.4 1.6 %copy.15 = bf16[1,16,4096]{2,1,0:T(8,128)(2,1)} copy(bf16[1,16,4096]{2,1,0:T(8,128)(2,1)} %bitcast.4) | data formatting | bytes 262144

commit v3 on v2

--- a/solution.py
+++ b/solution.py
@@ -193,10 +193,10 @@
         score = lax.dot_general(
             qrot[pl.ds(h * LOCAL, LOCAL), :], krot[...], (((1,), (1,)), ((), ())),
             preferred_element_type=F32,
-        ) / jnp.sqrt(F32(HEAD))
+        ) * F32(HEAD**-0.5)
         score = jnp.where(causal, score, F32(-1e30))
         peak = jnp.max(score, axis=-1, keepdims=True)
-        expon = jnp.where(causal, jnp.exp(score - peak), F32(0.0))
+        expon = jnp.exp(score - peak)
         total = jnp.sum(expon, axis=-1, keepdims=True)
         summed = jnp.dot(expon.astype(BF16), values, preferred_element_type=F32)
         attended.append((summed / total).astype(BF16))
@@ -268,14 +268,21 @@
     def p1_wait(p):
         wait(xs[p].at[0, 0, 0, pl.ds(0, 3)], p1r.at[p])
 
+    def p2_ahead(p):
+        b = ORDER[p][1]
+        block = at(xs[p], (k,), (0, W), me)
+        for step in (2, 1, 3):
+            send(block, block, device(me, k, b, step), p2s.at[p], p2r.at[p, 3])
+
     def p2_start(p, r):
         a, b, c = ORDER[p]
-        unit = at(xs[p], (k,), AG_ROUNDS[r], {b: me[b], c: me[c]})
         for step in (2, 1, 3):
-            send(unit, unit, device(me, k, b, step), p2s.at[p, r], p2r.at[p, r])
+            for other in (1, 2, 3):
+                unit = at(xs[p], (k,), AG_ROUNDS[r], {**me, a: (me[a] + other) % 4})
+                send(unit, unit, device(me, k, b, step), p2s.at[p], p2r.at[p, r])
 
     def p2_bytes(p, r):
-        return xs[p].at[0, 0, pl.ds(0, 3), :, :, pl.ds(*AG_ROUNDS[r])]
+        return xs[p].at[0, 0, pl.ds(0, 3), pl.ds(0, 3), :, pl.ds(*AG_ROUNDS[r])]
 
     def p3_unit(p, r, step, half=None):
         a, b, c = ORDER[p]
@@ -287,14 +294,16 @@
     def p3_send(p, r, step, half, way):
         unit = p3_unit(p, r, step, half)
         recv = p3r.at[p, r, 2] if half is not None else p3r.at[p, r, 0 if way == 1 else 1]
-        send(unit, unit, device(me, k, ORDER[p][2], way), p3s.at[p, r], recv)
+        send(unit, unit, device(me, k, ORDER[p][2], way), p3s.at[p], recv)
 
     def twin_send(p, r, step):
         unit = p3_unit(p, r, step)
-        send(unit, unit, twin, ds.at[p, r], dr.at[p, r])
+        send(unit, unit, twin, ds.at[p], dr.at[p, r])
 
     def p3_start(r):
         for p in PARTS:
+            if r == 0:
+                wait(xs[p].at[0, 0, 0, pl.ds(0, 3)], p2r.at[p, 3])
             wait(p2_bytes(p, r), p2r.at[p, r])
             p3_send(p, r, 0, None, 1)
             p3_send(p, r, 0, None, -1)
@@ -375,33 +384,28 @@
 
         lax.fori_loop(0, 8, one, 0, unroll=True)
 
-    def compact(r):
+    def compact(r, half):
         for p, lo, size, col in spans(r):
-            def one(g, carry, p=p, lo=lo, size=size, col=col):
-                tokens = xs[p][g // 4, g % 4, :, :, :, lo : lo + size].reshape(GROUP, size)
-                rows = jnp.dot(pick[g], tokens, preferred_element_type=F32).astype(BF16)
+            for z in range(4):
+                tokens = xs[p][half, z, :, :, :, lo : lo + size].reshape(GROUP, size)
+                rows = jnp.dot(pick[4 * half + z], tokens, preferred_element_type=F32).astype(BF16)
                 for e in range(2):
-                    packed[e, pl.ds(g * SLOTS, SLOTS), col : col + size] = rows[e * SLOTS : (e + 1) * SLOTS]
-                return carry
-
-            lax.fori_loop(0, 8, one, 0, unroll=True)
-
-    def gate_up(r):
-        def one(e, carry):
-            depth = sum(size for p, lo, size, col in spans(r))
+                    span = pl.ds((4 * half + z) * SLOTS, SLOTS)
+                    packed[e, span, col : col + size] = rows[e * SLOTS : (e + 1) * SLOTS]
+
+    def gate_up(r, rows):
+        depth = sum(size for p, lo, size, col in spans(r))
+        for e in range(2):
             total = jnp.dot(
-                packed[e, :, :depth], wgu[r % 2, e, :depth, :], preferred_element_type=F32
+                packed[e, rows, :depth], wgu[r % 2, e, :depth, :], preferred_element_type=F32
             )
             if r > 0:
-                total = total + acc[e]
+                total = total + acc[e, rows]
             if r < len(AG_ROUNDS) - 1:
-                acc[e] = total
+                acc[e, rows] = total
             else:
                 gate, up = total[:, :FF], total[:, FF:]
-                hidden[e] = (gate / (1.0 + jnp.exp(-gate)) * up).astype(BF16)
-            return carry
-
-        lax.fori_loop(0, 2, one, 0, unroll=True)
+                hidden[e, rows] = (gate / (1.0 + jnp.exp(-gate)) * up).astype(BF16)
 
 
     def out_cols(p, r):
@@ -411,30 +415,42 @@
         return lo, size
 
     def down(r):
+        def scatter(p, half):
+            lo, size = out_cols(p, r)
+
+            def one(i, carry):
+                g = 4 * half + i
+                rows = jnp.concatenate(
+                    [
+                        packed[e, pl.ds(g * SLOTS, SLOTS), 512 * p : 512 * p + size]
+                        for e in range(2)
+                    ],
+                    axis=0,
+                )
+                tokens = jnp.dot(unpick[g], rows, preferred_element_type=F32).astype(BF16)
+                xs[p][half, i, :, :, :, lo : lo + size] = tokens.reshape(4, 4, TOK, size)
+                return carry
+
+            lax.fori_loop(0, 4, one, 0, unroll=True)
+
+        def to_twin(p, step):
+            src = unit_of(xs[p], (1 - k,), p, r, step)
+            recv = qdr.at[p, r, 0 if step == 2 else 1]
+            send(src, unit_of(rd[p], (), p, r, step), twin, qds.at[p], recv)
+
         for p in PARTS:
             lo, size = out_cols(p, r)
             col = p * W + lo - GATES
-
-            def product(e, carry, lo=lo, size=size, col=col):
+            for e in range(2):
                 part = jnp.dot(hidden[e], wd[e, :, col : col + size], preferred_element_type=F32)
-                packed[e, :, :size] = (part * row_gate[e, :, 0:1]).astype(BF16)
-                return carry
-
-            lax.fori_loop(0, 2, product, 0, unroll=True)
-
-            def one(i, carry, p=p, lo=lo, size=size):
-                g = (i + 4 * (1 - k)) % 8
-                rows = jnp.concatenate(
-                    [packed[e, pl.ds(g * SLOTS, SLOTS), :size] for e in range(2)], axis=0
-                )
-                tokens = jnp.dot(unpick[g], rows, preferred_element_type=F32).astype(BF16)
-                xs[p][g // 4, g % 4, :, :, :, lo : lo + size] = tokens.reshape(4, 4, TOK, size)
-                return carry
-
-            lax.fori_loop(0, 4, one, 0, unroll=True)
-            cols = (lo, size)
-            send(at(xs[p], (1 - k,), cols, {}), at(rd[p], (), cols, {}), twin, qds.at[p, r], qdr.at[p, r])
-            lax.fori_loop(4, 8, one, 0, unroll=True)
+                packed[e, :, 512 * p : 512 * p + size] = (part * row_gate[e, :, 0:1]).astype(BF16)
+            scatter(p, 1 - k)
+            to_twin(p, 2)
+        for p in PARTS:
+            for step in (1, 3, 0):
+                to_twin(p, step)
+        for p in PARTS:
+            scatter(p, k)
 
     def total_into(dst, refs):
         total = refs[0][...].astype(F32)
@@ -464,20 +480,20 @@
         index = [fix.get(axis, slice(None)) for axis in "zyx" if axis != c]
         return ref.at[(*lead, *index, slice(None), pl.ds(*out_cols(p, r)))]
 
-    def halves(p, half):
-        return 2 * half
-
-    def s1(r):
-        for p in PARTS:
-            cols = out_cols(p, r)
-            wait(at(rd[p], (), cols, {}), qdr.at[p, r])
+    def a1(r):
+        for p in PARTS:
+            c = ORDER[p][2]
+            wait(unit_of(rd[p], (), p, r, 2), qdr.at[p, r, 0])
             add_unit(p, r, 2)
-            c = ORDER[p][2]
             for half, way in ((0, 1), (1, -1)):
                 src = unit_of(xs[p], (k,), p, r, 2, 2, half)
-                send(src, half_slot(p, r, half), device(me, k, c, way), qfs.at[p, r], qfr.at[p, r, half])
-            add_unit(p, r, 1)
-            add_unit(p, r, -1)
+                send(src, half_slot(p, r, half), device(me, k, c, way), qfs.at[p], qfr.at[p, r, half])
+
+    def b1(r):
+        for p in PARTS:
+            wait(at(rd[p], (), out_cols(p, r), {"z": pl.ds(0, 3)}), qdr.at[p, r, 1])
+            for step in (1, 3, 0):
+                add_unit(p, r, step)
 
     def half_slot(p, r, half, i=None):
         b = ORDER[p][1]
@@ -500,8 +516,7 @@
                 lax.fori_loop(0, 2, one, 0, unroll=True)
                 src = unit_of(xs[p], (k,), p, r, way)
                 slot = piece_of(rr[p], (half,), p, r, {})
-                send(src, slot, device(me, k, c, way), q3s.at[p, r], q3r.at[p, r])
-            add_unit(p, r, 0)
+                send(src, slot, device(me, k, c, way), q3s.at[p], q3r.at[p, r])
 
     def s3(r):
         for p in PARTS:
@@ -517,7 +532,7 @@
             for step in (2, 1, 3):
                 src = unit_of(xs[p], (k,), p, r, 0, 4, (me[b] + step) % 4)
                 slot = rb[p].at[step - 1, :, :, pl.ds(*out_cols(p, r))]
-                send(src, slot, device(me, k, b, step), q2s.at[p, r], q2r.at[p, r])
+                send(src, slot, device(me, k, b, step), q2s.at[p], q2r.at[p, r])
 
     def s4(r):
         for p in PARTS:
@@ -528,7 +543,7 @@
             total_into(mine, [mine] + [rb[p].at[j, :, :, cols] for j in range(3)])
             for step in (2, 1, 3):
                 src = at(xs[p], (k,), out_cols(p, r), {**me, a: (me[a] + step) % 4})
-                send(src, ra[p].at[step - 1, :, cols], device(me, k, a, step), q1s.at[p, r], q1r.at[p, r])
+                send(src, ra[p].at[step - 1, :, cols], device(me, k, a, step), q1s.at[p], q1r.at[p, r])
 
     def s5(r):
         for p in PARTS:
@@ -547,6 +562,8 @@
     p1_start(2)
     gates()
     p1_start(0)
+    for p in (1, 2, 0):
+        p2_ahead(p)
     for p in (1, 2, 0):
         p1_wait(p)
         for r in range(3):
@@ -559,37 +576,43 @@
     twin_wait(0)
     selections()
     p3_forward(1)
-    compact(0)
+    everything = pl.ds(0, 8 * SLOTS)
+    compact(0, 0)
+    compact(0, 1)
     weights_wait(0)
-    gate_up(0)
+    gate_up(0, everything)
     weights_start(2)
     p3_finish(1)
     p3_forward(2)
     twin_wait(1)
-    compact(1)
+    compact(1, 0)
+    compact(1, 1)
     weights_wait(1)
-    gate_up(1)
+    gate_up(1, everything)
     p3_finish(2)
-    twin_wait(2)
-    compact(2)
     weights_wait(2)
-    gate_up(2)
+    for half in (k, 1 - k):
+        if half is not k:
+            twin_wait(2)
+        compact(2, half)
+        gate_up(2, pl.ds(pl.multiple_of(half * 4 * SLOTS, 4 * SLOTS), 4 * SLOTS))
     load_down.wait()
     for p in PARTS:
         wait(xs[p].at[0, 0, 0, pl.ds(0, 3)], p1s.at[p])
-        for r in range(3):
-            cols = pl.ds(*AG_ROUNDS[r])
-            wait(p2_bytes(p, r), p2s.at[p, r])
-            wait(xs[p].at[0, pl.ds(0, 3), :, :, :, cols], p3s.at[p, r])
-            wait(xs[p].at[0, :, :, :, :, cols], ds.at[p, r])
+        wait(xs[p].at[0, 0, pl.ds(0, 3)], p2s.at[p])
+        wait(xs[p].at[0, pl.ds(0, 3)], p3s.at[p])
+        wait(xs[p].at[0], ds.at[p])
     down(0)
+    a1(0)
     down(1)
-    s1(0)
+    b1(0)
+    a1(1)
+    s2(0)
     down(2)
-    s1(1)
-    s2(0)
-    s1(2)
+    b1(1)
+    a1(2)
     s2(1)
+    b1(2)
     s3(0)
     s2(2)
     s4(0)
@@ -604,13 +627,13 @@
     for i in range(2):
         wait(from_ring.at[:, :, pl.ds(i * 2048, 2048)], ring_send.at[i])
     for p in PARTS:
-        for r in range(3):
-            cols = pl.ds(*out_cols(p, r))
-            wait(xs[p].at[0, :, :, :, :, cols], qds.at[p, r])
-            wait(rf[p].at[:, :, :, :, cols], qfs.at[p, r])
-            wait(rr[p].at[:, :, :, :, cols], q3s.at[p, r])
-            wait(rb[p].at[:, :, :, cols], q2s.at[p, r])
-            wait(ra[p].at[:, :, cols], q1s.at[p, r])
+        first = out_cols(p, 0)[0]
+        cols = pl.ds(first, W - first)
+        wait(xs[p].at[0, :, :, :, :, cols], qds.at[p])
+        wait(rf[p].at[:, :, :, :, cols], qfs.at[p])
+        wait(rr[p].at[:, :, :, :, cols], q3s.at[p])
+        wait(rb[p].at[:, :, :, cols], q2s.at[p])
+        wait(ra[p].at[:, :, cols], q1s.at[p])
 
 
 def on_device(
@@ -630,6 +653,7 @@
     hbm = pl.BlockSpec(memory_space=pl.ANY)
     dma = pltpu.SemaphoreType.DMA
     cosine, sine = rope_tables()
+    n = len(RS_ROUNDS)
 
     def half_shape(p):
         a, b, c = ORDER[p]
@@ -669,10 +693,10 @@
             vmem((2, 8 * SLOTS, 128), F32),
         ]
         + [dma((11,)), dma, dma, dma((2,)), dma((2,)), dma((2,)), dma((2,))]
-        + [dma((4,)), dma((3,)), dma((3,)), dma((3, 3)), dma((3, 3)), dma((3, 3)), dma((3, 3, 3))]
-        + [dma((3, 3)), dma((3, 3))]
-        + [dma((3, 3)), dma((3, 3)), dma((3, 3)), dma((3, 3, 2))]
-        + [dma((3, 3))] * 6
+        + [dma((4,)), dma((3,)), dma((3,)), dma((3,)), dma((3, 4)), dma((3,)), dma((3, 3, 3))]
+        + [dma((3,)), dma((3, 3))]
+        + [dma((3,)), dma((3, n, 2)), dma((3,)), dma((3, n, 2))]
+        + [dma((3,)), dma((3, n))] * 3
     )
     out = pl.pallas_call(
         layer_kernel,

time: 125 us -> 118 us (0.944)
  Pallas kernels: 123 us -> 117 us
    pallas_call x1, Pallas kernels: 123 us -> 117 us  [on_device(): pl.pallas_call(layer_kernel, out_shape=jax.ShapeDtypeStruct((TOK, D), BF1...]
where the time goes in v3:
time: 118 us
  Pallas kernels  117 us (99%)
  local copies, waits for them, and re-layouts  1.57 us (1%)
    pallas_call x1, Pallas kernels, on_device(): pl.pallas_call(layer_kernel, out_shape=jax.ShapeDtypeStruct((TOK, D), BF1...  117 us

profile of v3, /device:TPU:0, one launch (start us, length us, event | category | flops | bytes accessed | tf_op | source)
XLA Modules:
  0.0 118.1 jit_solution(253821938470290798)
XLA Ops:
  0.0 116.5 %shard_map.127 = bf16[16,4096]{1,0:T(8,128)(2,1)} custom-call(bf16[1,128,512]{2,1,0:T(8,128)(2,1)} %query_hbm.1, bf16[1,128,256]{2,1,0:T(8,128)(2,1)} %key_hbm.1, bf16[1,128,256]{2,1,0:T(8,128)(2,1)} %value_hbm.1, bf16[1,16,4096]{2,1,0:T(8,128)(2,1)} %residual_hbm.1, bf16[512,4096]{1,0:T(8,128)(2,1)} %proj_hbm.1, bf16[32,128]{1,0:T(8,128)(2,1)} %bitcast.6, ...), custom_call_target="tpu_custom_call" | custom-call | tf_op jit(solution)/shard_map/pallas_call | solution.py:701
  116.5 1.6 %copy.15 = bf16[1,16,4096]{2,1,0:T(8,128)(2,1)} copy(bf16[1,16,4096]{2,1,0:T(8,128)(2,1)} %bitcast.4) | data formatting | bytes 262144

commit v4 on v3

--- a/solution.py
+++ b/solution.py
@@ -27,7 +27,7 @@
 
 ORDER = (("x", "y", "z"), ("y", "z", "x"), ("z", "x", "y"))
 PARTS = range(3)
-AG_ROUNDS = ((0, 512), (512, 512), (1024, 384))
+AG_ROUNDS = ((0, 384), (384, 512), (896, 512))
 RS_ROUNDS = ((0, 384), (384, 512), (896, 512))
 VMEM = 63 * 2**20
 
@@ -212,11 +212,11 @@
         for v in range(4):
             rows = pl.ds(pl.multiple_of((c % 4) * LOCAL + (2 * v + 1 - k) * TOK, TOK), TOK)
             far[v, :, cols] = acc[c // 4, rows, :512].astype(BF16)
-        if c % 4 == 3:
-            half = pl.ds((c // 4) * 2048, 2048)
+        if c % 2 == 1:
+            half = pl.ds((c // 2) * 1024, 1024)
             send(
                 far.at[:, :, half], from_sibling.at[:, :, half], twin,
-                sib_send.at[c // 4], sib_recv.at[c // 4],
+                sib_send.at[c // 2], sib_recv.at[c // 2],
             )
     load_down.start()
 
@@ -224,13 +224,13 @@
         rows = pl.ds(pl.multiple_of((c % 4) * LOCAL + (2 * v + k) * TOK, TOK), TOK)
         return acc[c // 4, rows, :512] + from_sibling[v, :, c * 512 : (c + 1) * 512].astype(F32)
 
-    for i in range(2):
-        half = pl.ds(i * 2048, 2048)
+    for i in range(4):
+        half = pl.ds(i * 1024, 1024)
         wait(far.at[:, :, half], sib_send.at[i])
         wait(from_sibling.at[:, :, half], sib_recv.at[i])
         for step in (2, 1, 3):
             v = (me["x"] + step) % 4
-            for c in range(4 * i, 4 * i + 4):
+            for c in range(2 * i, 2 * i + 2):
                 far[v, :, c * 512 : (c + 1) * 512] = chip_sum(v, c).astype(BF16)
             send(
                 far.at[v, :, half], from_ring.at[step - 1, :, half], device(me, k, "x", step),
@@ -239,8 +239,8 @@
     square = jnp.zeros((TOK, 1), F32)
     for c in range(8):
         cols = slice(c * 512, (c + 1) * 512)
-        if c % 4 == 0:
-            wait(from_ring.at[:, :, pl.ds((c // 4) * 2048, 2048)], ring_recv.at[c // 4])
+        if c % 2 == 0:
+            wait(from_ring.at[:, :, pl.ds((c // 2) * 1024, 1024)], ring_recv.at[c // 2])
         projected = chip_sum(me["x"], c)
         for j in range(3):
             projected = projected + from_ring[j, :, cols].astype(F32)
@@ -624,8 +624,8 @@
     s4(2)
     s5(2)
     wait(kv.at[pl.ds(0, 3)], kv_send)
-    for i in range(2):
-        wait(from_ring.at[:, :, pl.ds(i * 2048, 2048)], ring_send.at[i])
+    for i in range(4):
+        wait(from_ring.at[:, :, pl.ds(i * 1024, 1024)], ring_send.at[i])
     for p in PARTS:
         first = out_cols(p, 0)[0]
         cols = pl.ds(first, W - first)
@@ -692,7 +692,7 @@
             vmem((8, GROUP, 2 * SLOTS), BF16),
             vmem((2, 8 * SLOTS, 128), F32),
         ]
-        + [dma((11,)), dma, dma, dma((2,)), dma((2,)), dma((2,)), dma((2,))]
+        + [dma((11,)), dma, dma, dma((4,)), dma((4,)), dma((4,)), dma((4,))]
         + [dma((4,)), dma((3,)), dma((3,)), dma((3,)), dma((3, 4)), dma((3,)), dma((3, 3, 3))]
         + [dma((3,)), dma((3, 3))]
         + [dma((3,)), dma((3, n, 2)), dma((3,)), dma((3, n, 2))]

time: 118 us -> 117 us (level)
  Pallas kernels: 117 us -> 115 us
    pallas_call x1, Pallas kernels: 117 us -> 115 us  [on_device(): pl.pallas_call(layer_kernel, out_shape=jax.ShapeDtypeStruct((TOK, D), BF1...]
where the time goes in v4:
time: 117 us
  Pallas kernels  115 us (98%)
  local copies, waits for them, and re-layouts  1.57 us (1%)
    pallas_call x1, Pallas kernels, on_device(): pl.pallas_call(layer_kernel, out_shape=jax.ShapeDtypeStruct((TOK, D), BF1...  115 us

profile of v4, /device:TPU:0, one launch (start us, length us, event | category | flops | bytes accessed | tf_op | source)
XLA Modules:
  0.0 116.6 jit_solution(4275659220617518583)
XLA Ops:
  0.0 115.0 %shard_map.127 = bf16[16,4096]{1,0:T(8,128)(2,1)} custom-call(bf16[1,128,512]{2,1,0:T(8,128)(2,1)} %query_hbm.1, bf16[1,128,256]{2,1,0:T(8,128)(2,1)} %key_hbm.1, bf16[1,128,256]{2,1,0:T(8,128)(2,1)} %value_hbm.1, bf16[1,16,4096]{2,1,0:T(8,128)(2,1)} %residual_hbm.1, bf16[512,4096]{1,0:T(8,128)(2,1)} %proj_hbm.1, bf16[32,128]{1,0:T(8,128)(2,1)} %bitcast.6, ...), custom_call_target="tpu_custom_call" | custom-call | tf_op jit(solution)/shard_map/pallas_call | solution.py:701
  115.0 1.6 %copy.15 = bf16[1,16,4096]{2,1,0:T(8,128)(2,1)} copy(bf16[1,16,4096]{2,1,0:T(8,128)(2,1)} %bitcast.4) | data formatting | bytes 262144

commit v5 on v4

--- a/solution.py
+++ b/solution.py
@@ -615,13 +615,13 @@
     b1(2)
     s3(0)
     s2(2)
+    s3(1)
     s4(0)
-    s3(1)
+    s3(2)
+    s4(1)
     s5(0)
-    s4(1)
-    s3(2)
+    s4(2)
     s5(1)
-    s4(2)
     s5(2)
     wait(kv.at[pl.ds(0, 3)], kv_send)
     for i in range(4):

time: 117 us -> 114 us (0.974)
  Pallas kernels: 115 us -> 113 us
    pallas_call x1, Pallas kernels: 115 us -> 113 us  [on_device(): pl.pallas_call(layer_kernel, out_shape=jax.ShapeDtypeStruct((TOK, D), BF1...]
where the time goes in v5:
time: 114 us
  Pallas kernels  113 us (99%)
  local copies, waits for them, and re-layouts  1.57 us (1%)
    pallas_call x1, Pallas kernels, on_device(): pl.pallas_call(layer_kernel, out_shape=jax.ShapeDtypeStruct((TOK, D), BF1...  113 us

profile of v5, /device:TPU:0, one launch (start us, length us, event | category | flops | bytes accessed | tf_op | source)
XLA Modules:
  0.0 114.2 jit_solution(6880472300415253174)
XLA Ops:
  0.0 112.6 %shard_map.127 = bf16[16,4096]{1,0:T(8,128)(2,1)} custom-call(bf16[1,128,512]{2,1,0:T(8,128)(2,1)} %query_hbm.1, bf16[1,128,256]{2,1,0:T(8,128)(2,1)} %key_hbm.1, bf16[1,128,256]{2,1,0:T(8,128)(2,1)} %value_hbm.1, bf16[1,16,4096]{2,1,0:T(8,128)(2,1)} %residual_hbm.1, bf16[512,4096]{1,0:T(8,128)(2,1)} %proj_hbm.1, bf16[32,128]{1,0:T(8,128)(2,1)} %bitcast.6, ...), custom_call_target="tpu_custom_call" | custom-call | tf_op jit(solution)/shard_map/pallas_call | solution.py:701
  112.6 1.6 %copy.15 = bf16[1,16,4096]{2,1,0:T(8,128)(2,1)} copy(bf16[1,16,4096]{2,1,0:T(8,128)(2,1)} %bitcast.4) | data formatting | bytes 262144

commit v6 on v5

--- a/solution.py
+++ b/solution.py
@@ -582,8 +582,8 @@
     weights_wait(0)
     gate_up(0, everything)
     weights_start(2)
+    p3_forward(2)
     p3_finish(1)
-    p3_forward(2)
     twin_wait(1)
     compact(1, 0)
     compact(1, 1)

time: 114 us -> 116 us (1.018)
  Pallas kernels: 113 us -> 115 us
    pallas_call x1, Pallas kernels: 113 us -> 115 us  [on_device(): pl.pallas_call(layer_kernel, out_shape=jax.ShapeDtypeStruct((TOK, D), BF1...]
where the time goes in v6:
time: 116 us
  Pallas kernels  115 us (99%)
  local copies, waits for them, and re-layouts  1.57 us (1%)
    pallas_call x1, Pallas kernels, on_device(): pl.pallas_call(layer_kernel, out_shape=jax.ShapeDtypeStruct((TOK, D), BF1...  115 us

profile of v6, /device:TPU:0, one launch (start us, length us, event | category | flops | bytes accessed | tf_op | source)
XLA Modules:
  0.0 116.3 jit_solution(12512796947536350346)
XLA Ops:
  0.0 114.7 %shard_map.127 = bf16[16,4096]{1,0:T(8,128)(2,1)} custom-call(bf16[1,128,512]{2,1,0:T(8,128)(2,1)} %query_hbm.1, bf16[1,128,256]{2,1,0:T(8,128)(2,1)} %key_hbm.1, bf16[1,128,256]{2,1,0:T(8,128)(2,1)} %value_hbm.1, bf16[1,16,4096]{2,1,0:T(8,128)(2,1)} %residual_hbm.1, bf16[512,4096]{1,0:T(8,128)(2,1)} %proj_hbm.1, bf16[32,128]{1,0:T(8,128)(2,1)} %bitcast.6, ...), custom_call_target="tpu_custom_call" | custom-call | tf_op jit(solution)/shard_map/pallas_call | solution.py:701
  114.7 1.6 %copy.15 = bf16[1,16,4096]{2,1,0:T(8,128)(2,1)} copy(bf16[1,16,4096]{2,1,0:T(8,128)(2,1)} %bitcast.4) | data formatting | bytes 262144
